TPU v7x, 32 devices: a whole 2x2x4 slice. The times are simulated.
32 devices in a mesh: groups: 2 (over y), ep: 4 (over z), role: 2 (over x), tp: 2 (over core).
Axes of the slice: x: 2, y: 2, z: 4, core: 2. Of those that a mesh axis runs over, the one named last changes fastest.
Arguments:
- moe_in: bfloat16 [128, 4096], P(('groups', 'ep', 'role'), 'tp'), parts along dimension 0, may hold values from -6 to 6
- expert_ids: int32 [128, 2], P(('groups', 'ep', 'role')), parts along dimension 0, may hold values from 0 to 3, all different within a row; in each aligned block of 8 rows (0 to 7, 8 to 15, ...) at most 6 rows name the same one
- gate_scores: float32 [128, 2], P(('groups', 'ep', 'role')), parts along dimension 0, may hold values from 0.05 to 0.5
- w_gate: bfloat16 [4, 4096, 1024], P('ep', 'tp', 'role'), may hold values from -0.09375 to 0.09375
- w_up: bfloat16 [4, 4096, 1024], P('ep', 'tp', 'role'), may hold values from -0.09375 to 0.09375
- w_down: bfloat16 [4, 1024, 4096], P('ep', None, ('role', 'tp')), may hold values from -0.1875 to 0.1875
- att_query: bfloat16 [64, 128, 576], P(('groups', 'ep', 'role'), 'tp'), parts along dimension 0, may hold values from -60 to 60
- att_cache: bfloat16 [64, 128, 576], P(('groups', 'ep', 'role')), parts along dimension 0, may hold values from -6 to 6
- cache_len: int32 [64], P(('groups', 'ep', 'role')), parts along dimension 0, may hold values from 2 to 128
Outputs:
- moe_out: bfloat16 [128, 4096], P(('groups', 'ep', 'role', 'tp')), parts along dimension 0
- att_out: bfloat16 [64, 128, 512], P(('groups', 'ep', 'role'), 'tp'), parts along dimension 0
There are 2 independent parts, one for each index of `groups`. A program takes and returns all parts, laid end to end along the dimension named above; an argument that names none is the same for every part. Nothing has to cross between parts.
Inputs may be any that keep to these rules, and one draw needn't show every extreme that they name: `expert_ids`: each row names 2 different experts; in each aligned block of 8 rows (the rows of one device along ep and role) no expert is named more than 6 times, a bound that some block reaches.
All inputs are finite; a program needn't handle non-finite values.
Results may differ from a plain program's by a relative error of at most 0.0085.
Values may be sent and summed in bfloat16 or wider, within the bound.
A program may use at most 64 MiB of HBM per device.

v0:
```python
import jax
import jax.numpy as jnp
from jax import lax
from jax.sharding import PartitionSpec as P

LAT = 512


score_scale = 192.0 ** (-0.5)


def slot_ranks(flat_ids):
    total_pairs = flat_ids.shape[0]
    matches = flat_ids[:, None] == flat_ids[None, :]
    indices = jnp.arange(total_pairs, dtype=jnp.int32)
    earlier = indices[None, :] < indices[:, None]
    return jnp.sum((matches & earlier).astype(jnp.int32), axis=1)


def latent_attention(queries, entries, lengths):
    scores = (
        jnp.einsum("rhc,rlc->rhl", queries, entries, preferred_element_type=jnp.float32)
        * score_scale
    )
    visible = jnp.arange(entries.shape[1], dtype=jnp.int32)[None, None, :] < lengths[:, None, None]
    scores = jnp.where(visible, scores, -1e30)
    highest = jnp.max(scores, axis=2, keepdims=True)
    weights = jnp.exp(scores - highest)
    chances = (weights / jnp.sum(weights, axis=2, keepdims=True)).astype(jnp.bfloat16)
    values = entries[:, :, :LAT]
    return jnp.einsum("rhl,rlc->rhc", chances, values, preferred_element_type=jnp.float32).astype(
        jnp.bfloat16
    )


def shards(moe_in, expert_ids, gate_scores, w_gate, w_up, w_down, att_query, att_cache, cache_len):
    att_out = latent_attention(att_query, att_cache, cache_len)
    row_count, half_width = moe_in.shape
    picks_row = expert_ids.shape[1]
    experts = lax.axis_size("ep")
    role_count = lax.axis_size("role")
    pair_count = lax.axis_size("tp")
    capacity = 3 * row_count * picks_row // (2 * experts)
    flat_ids = expert_ids.reshape(-1)
    target = flat_ids * capacity + slot_ranks(flat_ids)
    slot_hits = (
        target[:, None] == jnp.arange(experts * capacity, dtype=jnp.int32)[None, :]
    ).astype(jnp.float32)
    slot_hits = slot_hits.reshape(row_count, picks_row, experts * capacity)
    placement = jnp.sum(slot_hits, axis=1).astype(jnp.bfloat16)
    weighting = jnp.sum(slot_hits * gate_scores[:, :, None], axis=1)
    packed = jnp.einsum("ws,wd->sd", placement, moe_in, preferred_element_type=jnp.float32)
    packed = packed.astype(jnp.bfloat16).reshape(experts, capacity, half_width)
    copies = jnp.broadcast_to(packed[:, None], (experts, role_count, capacity, half_width))
    copies = copies.reshape(experts * role_count, capacity, half_width)
    arrived = lax.all_to_all(copies, ("ep", "role"), split_axis=0, concat_axis=0, tiled=True)
    gathered_rows = arrived.reshape(experts * role_count * capacity, half_width)
    gate_part = jnp.dot(gathered_rows, w_gate[0], preferred_element_type=jnp.float32)
    up_part = jnp.dot(gathered_rows, w_up[0], preferred_element_type=jnp.float32)
    down_local = w_down[0]
    gate_all, up_all = lax.psum((gate_part, up_part), "tp")
    hidden = (jax.nn.silu(gate_all) * up_all).astype(jnp.bfloat16)
    produced = jnp.dot(
        lax.all_gather(hidden, "role", axis=1, tiled=True),
        down_local,
        preferred_element_type=jnp.float32,
    )
    result = produced.astype(jnp.bfloat16).reshape(
        experts, role_count, capacity, down_local.shape[1]
    )
    returned = lax.all_to_all(result, "ep", split_axis=0, concat_axis=0, tiled=True)
    all_weights = lax.all_gather(weighting, "role", axis=0, tiled=True)
    all_weights = all_weights.reshape(role_count, row_count, experts, capacity)
    combined = jnp.einsum("qwec,eqcd->qwd", all_weights, returned.astype(jnp.float32))
    split_rows = combined.astype(jnp.bfloat16).reshape(
        role_count * pair_count, row_count // pair_count, down_local.shape[1]
    )
    moe_out = lax.all_to_all(
        split_rows, ("role", "tp"), split_axis=0, concat_axis=2, tiled=True
    ).reshape(row_count // pair_count, -1)
    return (moe_out, att_out)


def solution(mesh):
    placed = (
        P(("groups", "ep", "role"), "tp"),
        P(("groups", "ep", "role"), None),
        P(("groups", "ep", "role"), None),
        P("ep", "tp", "role"),
        P("ep", "tp", "role"),
        P("ep", None, ("role", "tp")),
        P(("groups", "ep", "role"), "tp", None),
        P(("groups", "ep", "role"), None, None),
        P(("groups", "ep", "role")),
    )
    return jax.shard_map(
        shards,
        mesh=mesh,
        in_specs=placed,
        out_specs=(
            P(("groups", "ep", "role", "tp"), None),
            P(("groups", "ep", "role"), "tp", None),
        ),
        check_vma=False,
    )
```

profile of v0, /device:TPU:0, one launch (start us, length us, event | category | flops | bytes accessed | tf_op | source)
XLA Modules:
  0.0 81.0 jit_solution(17733826257811013348)
XLA Ops:
  7.2 0.9 %copy.33 = s32[8,2]{1,0:T(8,128)S(1)} copy(s32[8,2]{0,1:T(2,128)} %param.10) | data formatting | bytes 128 | tf_op args[1]
  8.2 0.2 convert_reduce_fusion.1
  8.5 0.1 copy.35
  8.6 0.8 select_reduce_fusion
  9.3 1.0 %convolution_convert_fusion = bf16[24,2048]{1,0:T(8,128)(2,1)S(1)} fusion(bf16[8,2048]{1,0:T(8,128)(2,1)} %param.9, bf16[8,24]{1,0:T(8,128)(2,1)S(1)} %get-tuple-element.3), kind=kOutput, calls=%fused_computation.1 | convolution fusion | flops 835584 | bytes 131456 | tf_op jit(solution)/shard_map/ws,wd->sd/dot_general | solution.py:52
  10.4 16.0 %all_to_all.25 = bf16[8,6,2048]{2,1,0:T(8,128)(2,1)S(1)} all-to-all(bf16[8,6,2048]{2,1,0:T(8,128)(2,1)S(1)} %bitcast.31), channel_id=1, replica_groups=mesh['groups'=2,'ep'=4,'role'=2,'tp'=2] {'ep','role'}, dimensions={0} | all-to-all | bytes 393216 | tf_op jit(solution)/shard_map/all_to_all | solution.py:56
  26.4 2.8 %fusion.3 = f32[48,512]{1,0:T(8,128)} fusion(bf16[48,2048]{1,0:T(8,128)(2,1)S(1)} %reshape.70, bf16[1,2048,512]{2,1,0:T(8,128)(2,1)} %param.13), kind=kOutput, calls=%fused_computation.4 | convolution fusion | flops 100663296 | bytes 2392064 | tf_op jit(solution)/shard_map/dot_general | solution.py:59
  29.3 1.1 %fusion.5 = f32[48,512]{1,0:T(8,128)} fusion(bf16[48,2048]{1,0:T(8,128)(2,1)S(1)} %reshape.70, bf16[1,2048,512]{2,1,0:T(8,128)(2,1)S(1)} %copy-done.1), kind=kOutput, calls=%fused_computation.6 | convolution fusion | flops 100663296 | bytes 2392064 | tf_op jit(solution)/shard_map/dot_general | solution.py:58
  30.5 17.2 %all-reduce.3.cloned.1.call-done = (f32[48,512]{1,0:T(8,128)}, f32[48,512]{1,0:T(8,128)}) async-done(((f32[48,512]{1,0:T(8,128)}, f32[48,512]{1,0:T(8,128)}), (f32[48,512]{1,0:T(8,128)}, f32[48,512]{1,0:T(8,128)})) %all-reduce.3.cloned.1.call-update) | async-done | bytes 196624 | tf_op jit(solution)/shard_map/psum | solution.py:61
  47.7 1.0 %multiply_convert_fusion = bf16[48,512]{1,0:T(8,128)(2,1)S(1)} fusion(f32[48,512]{1,0:T(8,128)} %get-tuple-element.4, f32[48,512]{1,0:T(8,128)} %get-tuple-element.5), kind=kLoop, calls=%fused_computation.19 | loop fusion | flops 147456 | bytes 245760 | tf_op jit(solution)/shard_map/convert_element_type | solution.py:62
  48.7 4.8 %all_gather.7 = bf16[48,1024]{1,0:T(8,128)(2,1)S(1)} all-gather(bf16[48,512]{1,0:T(8,128)(2,1)S(1)} %multiply_convert_fusion), channel_id=1, replica_groups=mesh['groups'=2,'ep'=4,'role'=2,'tp'=2] {'role'}, dimensions={1}, use_global_device_ids=true | all-gather | bytes 147456 | tf_op jit(solution)/shard_map/all_gather | solution.py:64
  53.5 0.5 fusion.8
  54.0 0.7 copy.37
  54.8 4.9 %all-to-all-start.1 = ((bf16[4,2,6,1024]{3,1,2,0:T(2,128)(2,1)}), bf16[4,2,6,1024]{3,1,2,0:T(2,128)(2,1)S(1)}, u32[]{:S(2)}, u32[]{:S(2)}) async-start(bf16[4,2,6,1024]{3,1,2,0:T(2,128)(2,1)} %copy.37), calls=%async_computation.1 | async-start | bytes 196608 | tf_op jit(solution)/shard_map/all_to_all | solution.py:71
  59.6 0.2 fusion.11
  59.9 4.3 %all_gather.6 = bf16[16,24]{1,0:T(8,128)(2,1)S(1)} all-gather(bf16[8,24]{1,0:T(8,128)(2,1)S(1)} %get-tuple-element.2), channel_id=1, replica_groups=mesh['groups'=2,'ep'=4,'role'=2,'tp'=2] {'role'}, dimensions={0}, use_global_device_ids=true | all-gather | bytes 1152 | tf_op jit(solution)/shard_map/all_gather | solution.py:72
  64.3 0.2 fusion.21
  64.5 1.0 %all-to-all-done.1 = bf16[4,2,6,1024]{3,1,2,0:T(2,128)(2,1)S(1)} async-done(((bf16[4,2,6,1024]{3,1,2,0:T(2,128)(2,1)}), bf16[4,2,6,1024]{3,1,2,0:T(2,128)(2,1)S(1)}, u32[]{:S(2)}, u32[]{:S(2)}) %all-to-all-start.1) | async-done | bytes 98336 | tf_op jit(solution)/shard_map/all_to_all | solution.py:71
  65.5 0.2 fusion.13
  65.7 0.7 reshape.72
  66.3 3.3 %all-to-all-start.2 = ((bf16[4,4,1024]{2,1,0:T(4,128)(2,1)}), bf16[4,4,1024]{2,1,0:T(4,128)(2,1)S(1)}, u32[]{:S(2)}, u32[]{:S(2)}) async-start(bf16[4,4,1024]{2,1,0:T(4,128)(2,1)} %reshape.72), calls=%async_computation.2 | async-start | bytes 65536 | tf_op jit(solution)/shard_map/all_to_all | solution.py:78
  69.6 1.3 %convolution_convert_fusion.1 = bf16[4,64,512]{2,1,0:T(8,128)(2,1)} fusion(bf16[4,128,576]{1,2,0:T(8,128)(2,1)S(1)} %copy-done.2, f32[4,64]{1,0:T(4,128)S(1)} %fusion.21, f32[4,64,128]{2,1,0:T(8,128)S(1)} %fusion.11), kind=kOutput, calls=%fused_computation.8 | convolution fusion | flops 33784192 | bytes 1050624 | tf_op jit(solution)/shard_map/rhl,rlc->rhc/dot_general | solution.py:31
  70.9 2.6 %all-to-all-done.2 = bf16[4,4,1024]{2,1,0:T(4,128)(2,1)S(1)} async-done(((bf16[4,4,1024]{2,1,0:T(4,128)(2,1)}), bf16[4,4,1024]{2,1,0:T(4,128)(2,1)S(1)}, u32[]{:S(2)}, u32[]{:S(2)}) %all-to-all-start.2) | async-done | bytes 32800 | tf_op jit(solution)/shard_map/all_to_all | solution.py:78
  73.5 0.6 copy.53
  (21 shorter events, 0.6 us)
Async XLA Ops:
  7.2 46.3 %copy-start = (bf16[1,1024,1024]{2,1,0:T(8,128)(2,1)S(1)}, bf16[1,1024,1024]{2,1,0:T(8,128)(2,1)}, u32[]{:S(2)}) copy-start(bf16[1,1024,1024]{2,1,0:T(8,128)(2,1)} %param.14) | copy-start | bytes 6291460
  7.2 40.6 %all-reduce.3.cloned.1.call-start = ((), (), s32[]{:S(2)}) async-start(), calls=%async_computation.3 | async-start | bytes 393216 | tf_op jit(solution)/shard_map/psum | solution.py:61
  26.4 2.9 %copy-start.1 = (bf16[1,2048,512]{2,1,0:T(8,128)(2,1)S(1)}, bf16[1,2048,512]{2,1,0:T(8,128)(2,1)}, u32[]{:S(2)}) copy-start(bf16[1,2048,512]{2,1,0:T(8,128)(2,1)} %param.12) | copy-start | bytes 6291460
  26.4 4.0 %copy-start.4 = (s32[4]{0:T(128)S(1)}, s32[4]{0:T(128)}, u32[]{:S(2)}) copy-start(s32[4]{0:T(128)} %param.17) | copy-start | bytes 52
  30.4 29.2 %copy-start.2 = (bf16[4,128,576]{1,2,0:T(8,128)(2,1)S(1)}, bf16[4,128,576]{1,2,0:T(8,128)(2,1)}, u32[]{:S(2)}) copy-start(bf16[4,128,576]{1,2,0:T(8,128)(2,1)} %param.16) | copy-start | bytes 1769476
  30.4 29.2 %copy-start.3 = (bf16[4,64,576]{2,1,0:T(8,128)(2,1)S(1)}, bf16[4,64,576]{2,1,0:T(8,128)(2,1)}, u32[]{:S(2)}) copy-start(bf16[4,64,576]{2,1,0:T(8,128)(2,1)} %param.15) | copy-start | bytes 884740
  54.8 10.7 %all-to-all-start.1 = ((bf16[4,2,6,1024]{3,1,2,0:T(2,128)(2,1)}), bf16[4,2,6,1024]{3,1,2,0:T(2,128)(2,1)S(1)}, u32[]{:S(2)}, u32[]{:S(2)}) async-start(bf16[4,2,6,1024]{3,1,2,0:T(2,128)(2,1)} %copy.37), calls=%async_computation.1 | async-start | bytes 196608 | tf_op jit(solution)/shard_map/all_to_all | solution.py:71
  66.3 7.2 %all-to-all-start.2 = ((bf16[4,4,1024]{2,1,0:T(4,128)(2,1)}), bf16[4,4,1024]{2,1,0:T(4,128)(2,1)S(1)}, u32[]{:S(2)}, u32[]{:S(2)}) async-start(bf16[4,4,1024]{2,1,0:T(4,128)(2,1)} %reshape.72), calls=%async_computation.2 | async-start | bytes 65536 | tf_op jit(solution)/shard_map/all_to_all | solution.py:78
Sparse Core Ops, SparseCore 0:
  30.5 17.1 all-reduce.2
where the time goes:
time: 81.5 us; the launch traced here: 81 us
  blocking collectives  25.1 us (31%)
  waiting for transfers between devices  20.9 us (26%)
  between operations  14.1 us (17%)
  starting transfers between devices  8.16 us (10%)
  matrix products  7.15 us (9%)
  local copies, waits for them, and re-layouts  3.43 us (4%)
  other arithmetic  2.2 us (3%)
    psum x1, waiting for transfers between devices, shards(): gate_all, up_all = lax.psum((gate_part, up_part), 'tp')  17.2 us
    all_to_all x1, blocking collectives, shards(): lax.all_to_all(copies, ('ep', 'role'), split_axis=0, concat_axis=0, tiled...  16 us
    all_to_all x1, starting transfers between devices, shards(): lax.all_to_all(result, 'ep', split_axis=0, concat_axis=0, tiled=True)  4.85 us
    all_gather x1, blocking collectives, shards(): lax.all_gather(hidden, 'role', axis=1, tiled=True)  4.77 us
    all_gather x1, blocking collectives, shards(): all_weights = lax.all_gather(weighting, 'role', axis=0, tiled=True)  4.34 us
    all_to_all x1, starting transfers between devices, shards(): lax.all_to_all(split_rows, ('role', 'tp'), split_axis=0, concat_axis=2, t...  3.26 us
    dot_general x1, matrix products, shards(): jnp.dot(gathered_rows, w_up[0], preferred_element_type=jnp.float32)  2.85 us
    all_to_all x1, waiting for transfers between devices, shards(): lax.all_to_all(split_rows, ('role', 'tp'), split_axis=0, concat_axis=2, t...  2.63 us
  transfers between devices with their start and end apart: 3, of which 3 were waited for; matrix products, arithmetic and copies ran while one was open for 2% of the time, Pallas kernels for 0%

commit v1 on v0

v1 whole, which is shorter than its diff:
```python
import functools

import jax
import jax.numpy as jnp
from jax import lax
from jax.experimental import pallas as pl
from jax.experimental.pallas import tpu as pltpu
from jax.sharding import PartitionSpec as P

LAT = 512
MESH = pl.DeviceIdType.MESH
score_scale = 192.0 ** (-0.5)


def body(
    sizes,
    x, ids, gates, wg, wu, wd, query, cache, lens,
    moe, att,
    rows, wgv, wuv, wdv, qv, cv, psend, precv, hid, outb, ret, attv, moev,
    load_sem, put_sem, d_send, d_recv, p_sem, h_send, h_recv, r_send, r_recv,
):
    n_ep, n_role, n_tp = sizes
    quad = n_role * n_tp
    blocks = n_ep * n_role
    total = blocks * n_tp
    ep, role, tp = lax.axis_index("ep"), lax.axis_index("role"), lax.axis_index("tp")
    me_block = ep * n_role + role
    me_quad = role * n_tp + tp
    me = me_block * n_tp + tp
    small = total <= 16
    row_dev, width = x.shape
    part = row_dev // n_tp
    half = wgv.shape[1] // n_tp
    att_rows = qv.shape[0]

    def peer(index):
        return {
            "ep": lax.div(index, quad),
            "role": lax.rem(lax.div(index, n_tp), n_role),
            "tp": lax.rem(index, n_tp),
        }

    def each(start, stop, step):
        def run(k, carry):
            step(k)
            return carry

        lax.fori_loop(start, stop, run, 0, unroll=small)

    barrier = pltpu.get_barrier_semaphore()

    def greet(k):
        pl.semaphore_signal(
            barrier, inc=1, device_id=peer(lax.rem(me + k, total)), device_id_type=MESH
        )

    each(1, total, greet)

    own = pltpu.make_async_copy(x, rows.at[me_block], load_sem.at[0])
    loads = [
        pltpu.make_async_copy(source, target, load_sem.at[1 + i])
        for i, (source, target) in enumerate(
            [(query, qv), (cache, cv), (wg, wgv), (wu, wuv), (wd, wdv)]
        )
    ]
    own.start()
    for load in loads:
        load.start()

    pl.semaphore_wait(barrier, total - 1)

    def dispatch(block, source):
        return pltpu.make_async_remote_copy(
            src_ref=x,
            dst_ref=rows.at[source],
            send_sem=d_send.at[block],
            recv_sem=d_recv.at[source],
            device_id=peer(block * n_tp + tp),
            device_id_type=MESH,
        )

    each(1, blocks, lambda k: dispatch(lax.rem(me_block + k, blocks), me_block).start())

    def attend(r):
        q, entries = qv[r], cv[r]
        scores = (
            jnp.dot(q, entries, preferred_element_type=jnp.float32) * score_scale
        )
        visible = lax.broadcasted_iota(jnp.int32, scores.shape, 1) < lens[r]
        scores = jnp.where(visible, scores, -1e30)
        weights = jnp.exp(scores - jnp.max(scores, axis=1, keepdims=True))
        chances = (weights / jnp.sum(weights, axis=1, keepdims=True)).astype(jnp.bfloat16)
        attv[r] = lax.dot_general(
            chances, entries[:LAT], (((1,), (1,)), ((), ())), preferred_element_type=jnp.float32
        ).astype(jnp.bfloat16)

    def put(r):
        return pltpu.make_async_copy(attv.at[r], att.at[r], put_sem.at[r])

    loads[0].wait()
    loads[1].wait()
    cut = att_rows // 2
    for r in range(cut):
        attend(r)
        put(r).start()

    loads[2].wait()
    loads[3].wait()
    own.wait()
    each(1, blocks, lambda k: dispatch(me_block, lax.rem(me_block + k, blocks)).wait_recv())

    gathered = (
        rows[...].astype(jnp.float32).reshape(blocks * row_dev, width).astype(jnp.bfloat16)
    )

    def column_sums(which):
        columns = pl.ds(pl.multiple_of(which * half, half), half)
        gate = jnp.dot(gathered, wgv[:, columns], preferred_element_type=jnp.float32)
        up = jnp.dot(gathered, wuv[:, columns], preferred_element_type=jnp.float32)
        return gate, up

    gate, up = column_sums(1 - tp)
    psend[0] = gate
    psend[1] = up
    swap = pltpu.make_async_remote_copy(
        src_ref=psend,
        dst_ref=precv,
        send_sem=p_sem.at[0],
        recv_sem=p_sem.at[1],
        device_id={"tp": 1 - tp},
        device_id_type=MESH,
    )
    swap.start()
    gate, up = column_sums(tp)
    swap.wait_recv()
    gate = gate + precv[0]
    up = up + precv[1]
    hid[me_quad] = (gate / (1.0 + jnp.exp(-gate)) * up).astype(jnp.bfloat16)

    def share(target, source):
        return pltpu.make_async_remote_copy(
            src_ref=hid.at[me_quad],
            dst_ref=hid.at[source],
            send_sem=h_send.at[target],
            recv_sem=h_recv.at[source],
            device_id={"role": lax.div(target, n_tp), "tp": lax.rem(target, n_tp)},
            device_id_type=MESH,
        )

    for k in range(1, quad):
        share(lax.rem(me_quad + k, quad), me_quad).start()

    for r in range(cut, att_rows):
        attend(r)
        put(r).start()

    loads[4].wait()
    produced = None
    for k in range(quad):
        source = lax.rem(me_quad + k, quad)
        if k:
            share(me_quad, source).wait_recv()
        span = pl.ds(pl.multiple_of(source * half, half), half)
        term = jnp.dot(hid[source], wdv[span, :], preferred_element_type=jnp.float32)
        produced = term if produced is None else produced + term

    outb[...] = produced.reshape(total, part, produced.shape[1]).astype(jnp.bfloat16)

    def give(target, source):
        return pltpu.make_async_remote_copy(
            src_ref=outb.at[target],
            dst_ref=ret.at[source],
            send_sem=r_send.at[target],
            recv_sem=r_recv.at[source],
            device_id=peer(target),
            device_id_type=MESH,
        )

    each(1, total, lambda k: give(lax.rem(me + k, total), me).start())
    keep = pltpu.make_async_copy(outb.at[me], ret.at[me], load_sem.at[0])
    keep.start()

    named, score = ids[...], gates[...]
    mine = lax.broadcasted_iota(jnp.int32, (part, row_dev), 1) == tp * part + (
        lax.broadcasted_iota(jnp.int32, (part, row_dev), 0)
    )
    table = []
    for e in range(n_ep):
        weight = jnp.sum(jnp.where(named == e, score, 0.0), axis=0, keepdims=True)
        table.append(jnp.sum(jnp.where(mine, weight, 0.0), axis=1, keepdims=True))

    keep.wait()
    each(1, total, lambda k: give(me, lax.rem(me + k, total)).wait_recv())

    columns = ret.shape[2]
    for j in range(quad):
        acc = None
        for e in range(n_ep):
            term = table[e] * ret[e * quad + j].astype(jnp.float32)
            acc = term if acc is None else acc + term
        moev[:, j * columns : (j + 1) * columns] = acc.astype(jnp.bfloat16)
    last = pltpu.make_async_copy(moev, moe, load_sem.at[1])
    last.start()

    each(1, blocks, lambda k: dispatch(lax.rem(me_block + k, blocks), me_block).wait_send())
    swap.wait_send()
    for k in range(1, quad):
        share(lax.rem(me_quad + k, quad), me_quad).wait_send()
    each(1, total, lambda k: give(lax.rem(me + k, total), me).wait_send())
    for r in range(att_rows):
        put(r).wait()
    last.wait()


def shards(sizes, moe_in, expert_ids, gate_scores, w_gate, w_up, w_down, att_query, att_cache, cache_len):
    n_ep, n_role, n_tp = sizes
    quad, blocks = n_role * n_tp, n_ep * n_role
    total = blocks * n_tp
    row_dev, width = moe_in.shape
    part = row_dev // n_tp
    hidden = w_gate.shape[2]
    units, columns = w_down.shape[1:]
    half = hidden // n_tp
    att_rows, heads, _ = att_query.shape
    entries = jnp.swapaxes(att_cache, 1, 2)
    bf16, f32 = jnp.bfloat16, jnp.float32
    anywhere = pl.BlockSpec(memory_space=pl.ANY)
    vmem = pl.BlockSpec(memory_space=pltpu.VMEM)
    smem = pl.BlockSpec(memory_space=pltpu.SMEM)
    dma = pltpu.SemaphoreType.DMA
    flops = 2 * blocks * row_dev * (2 * width * hidden + units * columns)
    return pl.pallas_call(
        functools.partial(body, sizes),
        out_shape=(
            jax.ShapeDtypeStruct((part, columns * quad), bf16),
            jax.ShapeDtypeStruct((att_rows, heads, LAT), bf16),
        ),
        in_specs=[anywhere, vmem, vmem] + [anywhere] * 5 + [smem],
        out_specs=(anywhere, anywhere),
        scratch_shapes=[
            pltpu.VMEM((blocks, row_dev, width), bf16),
            pltpu.VMEM((width, hidden), bf16),
            pltpu.VMEM((width, hidden), bf16),
            pltpu.VMEM((units, columns), bf16),
            pltpu.VMEM(att_query.shape, bf16),
            pltpu.VMEM(entries.shape, bf16),
            pltpu.VMEM((2, blocks * row_dev, half), f32),
            pltpu.VMEM((2, blocks * row_dev, half), f32),
            pltpu.VMEM((quad, blocks * row_dev, half), bf16),
            pltpu.VMEM((total, part, columns), bf16),
            pltpu.VMEM((total, part, columns), bf16),
            pltpu.VMEM((att_rows, heads, LAT), bf16),
            pltpu.VMEM((part, columns * quad), bf16),
            dma((6,)),
            dma((att_rows,)),
            dma((blocks,)),
            dma((blocks,)),
            dma((2,)),
            dma((quad,)),
            dma((quad,)),
            dma((total,)),
            dma((total,)),
        ],
        compiler_params=pltpu.CompilerParams(
            collective_id=0, has_side_effects=True, vmem_limit_bytes=56 * 1024 * 1024
        ),
        cost_estimate=pl.CostEstimate(flops=flops, bytes_accessed=8 << 20, transcendentals=0),
    )(
        moe_in, expert_ids.T, gate_scores.T, w_gate[0], w_up[0], w_down[0], att_query, entries, cache_len
    )


def solution(mesh):
    placed = (
        P(("groups", "ep", "role"), "tp"),
        P(("groups", "ep", "role"), None),
        P(("groups", "ep", "role"), None),
        P("ep", "tp", "role"),
        P("ep", "tp", "role"),
        P("ep", None, ("role", "tp")),
        P(("groups", "ep", "role"), "tp", None),
        P(("groups", "ep", "role"), None, None),
        P(("groups", "ep", "role")),
    )
    sizes = (mesh.shape["ep"], mesh.shape["role"], mesh.shape["tp"])
    return jax.shard_map(
        functools.partial(shards, sizes),
        mesh=mesh,
        in_specs=placed,
        out_specs=(
            P(("groups", "ep", "role", "tp"), None),
            P(("groups", "ep", "role"), "tp", None),
        ),
        check_vma=False,
    )
```

time: 81.5 us -> 29.2 us (0.36)
  Pallas kernels: 0 us -> 25.3 us
  blocking collectives: 25.1 us -> 0 us
  waiting for transfers between devices: 20.9 us -> 0 us
  between operations: 14.1 us -> 0.64 us
  starting transfers between devices: 8.16 us -> 0 us
  matrix products: 7.15 us -> 0 us
  other arithmetic: 2.2 us -> 0 us
    pallas_call x0 -> x1, Pallas kernels: none -> 25.3 us  [shards(): pl.pallas_call(functools.partial(body, sizes), out_shape=(jax.ShapeDtypeS...]
    psum x1 -> x0, waiting for transfers between devices: 17.2 us -> none  [shards(): gate_all, up_all = lax.psum((gate_part, up_part), 'tp')]
    all_to_all x1 -> x0, blocking collectives: 16 us -> none  [shards(): lax.all_to_all(copies, ('ep', 'role'), split_axis=0, concat_axis=0, tiled...]
    all_gather x2 -> x0, blocking collectives: 9.11 us -> none  [the longest x1 4.77 us: shards(): lax.all_gather(hidden, 'role', axis=1, tiled=True)]
    all_to_all x2 -> x0, starting transfers between devices: 8.12 us -> none  [the longest x1 4.85 us: shards(): lax.all_to_all(result, 'ep', split_axis=0, concat_axis=0, tiled=True)]
    dot_general x7 -> x0, matrix products: 7.15 us -> none  [the longest x1 2.85 us: shards(): jnp.dot(gathered_rows, w_up[0], preferred_element_type=jnp.float32)]
    all_to_all x2 -> x0, waiting for transfers between devices: 3.59 us -> none  [the longest x1 2.63 us: shards(): lax.all_to_all(split_rows, ('role', 'tp'), split_axis=0, concat_axis=2, t...]
    reshape x5 -> x0, local copies, waits for them, and re-layouts: 1.58 us -> none  [the longest x2 0.78 us: shards(): produced.astype(jnp.bfloat16)]
  transfers between devices with their start and end apart: 3 -> 0, of which waited for: 3 -> 0; matrix products, arithmetic and copies ran while one was open for 2% -> 0% of each run, Pallas kernels for 0% -> 0%
where the time goes in v1:
time: 29.2 us; the launch traced here: 29 us
  Pallas kernels  25.3 us (87%)
  local copies, waits for them, and re-layouts  3.05 us (10%)
  between operations  0.64 us (2%)
    pallas_call x1, Pallas kernels, shards(): pl.pallas_call(functools.partial(body, sizes), out_shape=(jax.ShapeDtypeS...  25.3 us
    unnamed x2, local copies, waits for them, and re-layouts  3.05 us

profile of v1, /device:TPU:0, one launch (start us, length us, event | category | flops | bytes accessed | tf_op | source)
XLA Modules:
  0.0 29.0 jit_solution(10481018902385373055)
XLA Ops:
  0.6 25.3 %shard_map.104 = (bf16[4,4096]{1,0:T(4,128)(2,1)}, bf16[4,64,512]{2,1,0:T(8,128)(2,1)}) custom-call(bf16[8,2048]{1,0:T(8,128)(2,1)} %x.1, s32[2,8]{1,0:T(2,128)} %bitcast.10, f32[2,8]{1,0:T(2,128)} %bitcast.11, bf16[2048,512]{1,0:T(8,128)(2,1)} %bitcast.6, bf16[2048,512]{1,0:T(8,128)(2,1)} %bitcast.7, bf16[1024,1024]{1,0:T(8,128)(2,1)} %bitcast.8, ...), custom_call_target="tpu_custom_call" | custom-call | flops 402653184 | bytes 8388608 | tf_op jit(solution)/shard_map/pallas_call | solution.py:232
  25.9 1.4 %copy.13 = bf16[4,4096]{1,0:T(4,128)(2,1)} copy(bf16[4,4096]{1,0:T(4,128)(2,1)} %get-tuple-element.4) | data formatting | bytes 65536
  27.3 1.7 %copy.14 = bf16[4,64,512]{2,1,0:T(8,128)(2,1)} copy(bf16[4,64,512]{2,1,0:T(8,128)(2,1)} %get-tuple-element.5) | data formatting | bytes 524288

commit v2 on v1

--- a/solution.py
+++ b/solution.py
@@ -229,7 +229,7 @@
     smem = pl.BlockSpec(memory_space=pltpu.SMEM)
     dma = pltpu.SemaphoreType.DMA
     flops = 2 * blocks * row_dev * (2 * width * hidden + units * columns)
-    return pl.pallas_call(
+    moe, att = pl.pallas_call(
         functools.partial(body, sizes),
         out_shape=(
             jax.ShapeDtypeStruct((part, columns * quad), bf16),
@@ -268,6 +268,28 @@
     )(
         moe_in, expert_ids.T, gate_scores.T, w_gate[0], w_up[0], w_down[0], att_query, entries, cache_len
     )
+    return settled(moe, att, pltpu.VMEM)
+
+
+def settle(a, b, out_a, out_b, sem):
+    first = pltpu.make_async_copy(a, out_a, sem.at[0])
+    second = pltpu.make_async_copy(b, out_b, sem.at[1])
+    second.start()
+    first.start()
+    second.wait()
+    first.wait()
+
+
+def settled(a, b, space):
+    anywhere = pl.BlockSpec(memory_space=pl.ANY)
+    inner = pl.BlockSpec(memory_space=space)
+    return pl.pallas_call(
+        settle,
+        out_shape=(jax.ShapeDtypeStruct(a.shape, a.dtype), jax.ShapeDtypeStruct(b.shape, b.dtype)),
+        in_specs=[inner, inner],
+        out_specs=(anywhere, anywhere),
+        scratch_shapes=[pltpu.SemaphoreType.DMA((2,))],
+    )(a, b)
 
 
 def solution(mesh):

time: 29.2 us -> 27.8 us (0.952)
  local copies, waits for them, and re-layouts: 3.05 us -> 0 us
  Pallas kernels: 25.3 us -> 27 us
    unnamed x2 -> x0, local copies, waits for them, and re-layouts: 3.05 us -> none
    pallas_call x0 -> x1, Pallas kernels: none -> 1.69 us  [settled(): pl.pallas_call(settle, out_shape=(jax.ShapeDtypeStruct(a.shape, a.dtype),...]
where the time goes in v2:
time: 27.8 us; the launch traced here: 27.6 us
  Pallas kernels  27 us (97%)
  between operations  0.64 us (2%)
    pallas_call x1, Pallas kernels, shards(): pl.pallas_call(functools.partial(body, sizes), out_shape=(jax.ShapeDtypeS...  25.3 us
    pallas_call x1, Pallas kernels, settled(): pl.pallas_call(settle, out_shape=(jax.ShapeDtypeStruct(a.shape, a.dtype),...  1.69 us

profile of v2, /device:TPU:0, one launch (start us, length us, event | category | flops | bytes accessed | tf_op | source)
XLA Modules:
  0.0 27.6 jit_solution(2484847585539209131)
XLA Ops:
  0.6 25.3 %shard_map.104 = (bf16[4,4096]{1,0:T(4,128)(2,1)}, bf16[4,64,512]{2,1,0:T(8,128)(2,1)}) custom-call(bf16[8,2048]{1,0:T(8,128)(2,1)} %x.1, s32[2,8]{1,0:T(2,128)} %bitcast.10, f32[2,8]{1,0:T(2,128)} %bitcast.11, bf16[2048,512]{1,0:T(8,128)(2,1)} %bitcast.6, bf16[2048,512]{1,0:T(8,128)(2,1)} %bitcast.7, bf16[1024,1024]{1,0:T(8,128)(2,1)} %bitcast.8, ...), custom_call_target="tpu_custom_call" | custom-call | flops 402653184 | bytes 8388608 | tf_op jit(solution)/shard_map/pallas_call | solution.py:232
  25.9 1.7 %shard_map.105 = (bf16[4,4096]{1,0:T(4,128)(2,1)}, bf16[4,64,512]{2,1,0:T(8,128)(2,1)}) custom-call(bf16[4,4096]{1,0:T(4,128)(2,1)} %get-tuple-element.4.a, bf16[4,64,512]{2,1,0:T(8,128)(2,1)} %get-tuple-element.5.b), custom_call_target="tpu_custom_call" | custom-call | tf_op jit(solution)/shard_map/pallas_call | solution.py:286

commit v3 on v2

--- a/solution.py
+++ b/solution.py
@@ -17,7 +17,7 @@
     x, ids, gates, wg, wu, wd, query, cache, lens,
     moe, att,
     rows, wgv, wuv, wdv, qv, cv, psend, precv, hid, outb, ret, attv, moev,
-    load_sem, put_sem, d_send, d_recv, p_sem, h_send, h_recv, r_send, r_recv,
+    load_sem, put_sem, d_send, d_recv, f_send, p_sem, h_send, h_recv, r_send, r_recv,
 ):
     n_ep, n_role, n_tp = sizes
     quad = n_role * n_tp
@@ -67,11 +67,12 @@
     for load in loads:
         load.start()
 
+    own.wait()
     pl.semaphore_wait(barrier, total - 1)
 
     def dispatch(block, source):
         return pltpu.make_async_remote_copy(
-            src_ref=x,
+            src_ref=rows.at[me_block],
             dst_ref=rows.at[source],
             send_sem=d_send.at[block],
             recv_sem=d_recv.at[source],
@@ -79,7 +80,35 @@
             device_id_type=MESH,
         )
 
-    each(1, blocks, lambda k: dispatch(lax.rem(me_block + k, blocks), me_block).start())
+    half_ep = n_ep // 2
+    near = lax.div(ep, half_ep) * half_ep
+    far = lax.rem(near + half_ep, n_ep)
+
+    def near_block(k):
+        return near * n_role + lax.rem(me_block - near * n_role + k, half_ep * n_role)
+
+    def far_ep(k):
+        return far + lax.rem(ep - near + k, half_ep)
+
+    def relay(source_ep, target, j):
+        block = source_ep * n_role + lax.rem(role + j, n_role) if j else source_ep * n_role + role
+        return pltpu.make_async_remote_copy(
+            src_ref=rows.at[block],
+            dst_ref=rows.at[block],
+            send_sem=f_send.at[source_ep * n_role + target],
+            recv_sem=d_recv.at[block],
+            device_id={"role": target},
+            device_id_type=MESH,
+        )
+
+    each(0, half_ep, lambda k: dispatch(far_ep(k) * n_role + role, me_block).start())
+    each(1, half_ep * n_role, lambda k: dispatch(near_block(k), me_block).start())
+
+    def pass_on(k):
+        source = far_ep(k)
+        dispatch(me_block, source * n_role + role).wait_recv()
+        for j in range(1, n_role):
+            relay(source, lax.rem(role + j, n_role), 0).start()
 
     def attend(r):
         q, entries = qv[r], cv[r]
@@ -103,11 +132,18 @@
     for r in range(cut):
         attend(r)
         put(r).start()
+        if r == 0:
+            each(0, half_ep, pass_on)
 
     loads[2].wait()
     loads[3].wait()
-    own.wait()
-    each(1, blocks, lambda k: dispatch(me_block, lax.rem(me_block + k, blocks)).wait_recv())
+    each(1, half_ep * n_role, lambda k: dispatch(me_block, near_block(k)).wait_recv())
+
+    def relayed(k):
+        for j in range(1, n_role):
+            relay(far_ep(k), role, j).wait_recv()
+
+    each(0, half_ep, relayed)
 
     gathered = (
         rows[...].astype(jnp.float32).reshape(blocks * row_dev, width).astype(jnp.bfloat16)
@@ -202,7 +238,14 @@
     last = pltpu.make_async_copy(moev, moe, load_sem.at[1])
     last.start()
 
-    each(1, blocks, lambda k: dispatch(lax.rem(me_block + k, blocks), me_block).wait_send())
+    each(0, half_ep, lambda k: dispatch(far_ep(k) * n_role + role, me_block).wait_send())
+    each(1, half_ep * n_role, lambda k: dispatch(near_block(k), me_block).wait_send())
+
+    def sent(k):
+        for j in range(1, n_role):
+            relay(far_ep(k), lax.rem(role + j, n_role), 0).wait_send()
+
+    each(0, half_ep, sent)
     swap.wait_send()
     for k in range(1, quad):
         share(lax.rem(me_quad + k, quad), me_quad).wait_send()
@@ -255,6 +298,7 @@
             dma((att_rows,)),
             dma((blocks,)),
             dma((blocks,)),
+            dma((blocks,)),
             dma((2,)),
             dma((quad,)),
             dma((quad,)),

time: 27.8 us -> 27 us (0.971)
  Pallas kernels: 27 us -> 26.2 us
    pallas_call x1, Pallas kernels: 25.3 us -> 24.5 us  [shards(): pl.pallas_call(functools.partial(body, sizes), out_shape=(jax.ShapeDtypeS...]
where the time goes in v3:
time: 27 us; the launch traced here: 26.8 us
  Pallas kernels  26.2 us (97%)
  between operations  0.64 us (2%)
    pallas_call x1, Pallas kernels, shards(): pl.pallas_call(functools.partial(body, sizes), out_shape=(jax.ShapeDtypeS...  24.5 us
    pallas_call x1, Pallas kernels, settled(): pl.pallas_call(settle, out_shape=(jax.ShapeDtypeStruct(a.shape, a.dtype),...  1.69 us

profile of v3, /device:TPU:0, one launch (start us, length us, event | category | flops | bytes accessed | tf_op | source)
XLA Modules:
  0.0 26.8 jit_solution(15795432118363935544)
XLA Ops:
  0.6 24.5 %shard_map.104 = (bf16[4,4096]{1,0:T(4,128)(2,1)}, bf16[4,64,512]{2,1,0:T(8,128)(2,1)}) custom-call(bf16[8,2048]{1,0:T(8,128)(2,1)} %x.1, s32[2,8]{1,0:T(2,128)} %bitcast.10, f32[2,8]{1,0:T(2,128)} %bitcast.11, bf16[2048,512]{1,0:T(8,128)(2,1)} %bitcast.6, bf16[2048,512]{1,0:T(8,128)(2,1)} %bitcast.7, bf16[1024,1024]{1,0:T(8,128)(2,1)} %bitcast.8, ...), custom_call_target="tpu_custom_call" | custom-call | flops 402653184 | bytes 8388608 | tf_op jit(solution)/shard_map/pallas_call | solution.py:275
  25.2 1.7 %shard_map.105 = (bf16[4,4096]{1,0:T(4,128)(2,1)}, bf16[4,64,512]{2,1,0:T(8,128)(2,1)}) custom-call(bf16[4,4096]{1,0:T(4,128)(2,1)} %get-tuple-element.4.a, bf16[4,64,512]{2,1,0:T(8,128)(2,1)} %get-tuple-element.5.b), custom_call_target="tpu_custom_call" | custom-call | tf_op jit(solution)/shard_map/pallas_call | solution.py:330

commit v4 on v3

--- a/solution.py
+++ b/solution.py
@@ -139,25 +139,35 @@
     loads[3].wait()
     each(1, half_ep * n_role, lambda k: dispatch(me_block, near_block(k)).wait_recv())
 
-    def relayed(k):
-        for j in range(1, n_role):
-            relay(far_ep(k), role, j).wait_recv()
-
-    each(0, half_ep, relayed)
-
-    gathered = (
-        rows[...].astype(jnp.float32).reshape(blocks * row_dev, width).astype(jnp.bfloat16)
-    )
-
-    def column_sums(which):
+    count = half_ep * n_role
+    lot = count * row_dev
+
+    def gather(first):
+        got = rows[pl.ds(first * n_role, count)]
+        return got.astype(jnp.float32).reshape(lot, width).astype(jnp.bfloat16)
+
+    def column_sums(gathered, which):
         columns = pl.ds(pl.multiple_of(which * half, half), half)
         gate = jnp.dot(gathered, wgv[:, columns], preferred_element_type=jnp.float32)
         up = jnp.dot(gathered, wuv[:, columns], preferred_element_type=jnp.float32)
         return gate, up
 
-    gate, up = column_sums(1 - tp)
-    psend[0] = gate
-    psend[1] = up
+    early = gather(near)
+    gate, up = column_sums(early, 1 - tp)
+    psend[0, :lot] = gate
+    psend[1, :lot] = up
+    near_gate, near_up = column_sums(early, tp)
+
+    def relayed(k):
+        for j in range(1, n_role):
+            relay(far_ep(k), role, j).wait_recv()
+
+    each(0, half_ep, relayed)
+
+    late = gather(far)
+    gate, up = column_sums(late, 1 - tp)
+    psend[0, lot:] = gate
+    psend[1, lot:] = up
     swap = pltpu.make_async_remote_copy(
         src_ref=psend,
         dst_ref=precv,
@@ -167,10 +177,10 @@
         device_id_type=MESH,
     )
     swap.start()
-    gate, up = column_sums(tp)
+    gate, up = column_sums(late, tp)
     swap.wait_recv()
-    gate = gate + precv[0]
-    up = up + precv[1]
+    gate = jnp.concatenate([near_gate, gate], axis=0) + precv[0]
+    up = jnp.concatenate([near_up, up], axis=0) + precv[1]
     hid[me_quad] = (gate / (1.0 + jnp.exp(-gate)) * up).astype(jnp.bfloat16)
 
     def share(target, source):
@@ -200,7 +210,9 @@
         term = jnp.dot(hid[source], wdv[span, :], preferred_element_type=jnp.float32)
         produced = term if produced is None else produced + term
 
-    outb[...] = produced.reshape(total, part, produced.shape[1]).astype(jnp.bfloat16)
+    produced = produced.reshape(total, part, produced.shape[1]).astype(jnp.bfloat16)
+    outb[pl.ds(near * quad, total // 2)] = produced[: total // 2]
+    outb[pl.ds(far * quad, total // 2)] = produced[total // 2 :]
 
     def give(target, source):
         return pltpu.make_async_remote_copy(
@@ -312,27 +324,38 @@
     )(
         moe_in, expert_ids.T, gate_scores.T, w_gate[0], w_up[0], w_down[0], att_query, entries, cache_len
     )
-    return settled(moe, att, pltpu.VMEM)
-
-
-def settle(a, b, out_a, out_b, sem):
-    first = pltpu.make_async_copy(a, out_a, sem.at[0])
-    second = pltpu.make_async_copy(b, out_b, sem.at[1])
-    second.start()
-    first.start()
-    second.wait()
-    first.wait()
-
-
-def settled(a, b, space):
+    return settled(moe, att)
+
+
+def settle(a, b, out_a, out_b, held_a, held_b, sem):
+    rows = b.shape[0]
+    inward = [pltpu.make_async_copy(a, held_a, sem.at[0, 0])]
+    outward = [pltpu.make_async_copy(held_a, out_a, sem.at[1, 0])]
+    for r in range(rows):
+        inward.append(pltpu.make_async_copy(b.at[r], held_b.at[r], sem.at[0, 1 + r]))
+        outward.append(pltpu.make_async_copy(held_b.at[r], out_b.at[r], sem.at[1, 1 + r]))
+    for copy in inward:
+        copy.start()
+    for copy, onward in zip(inward, outward):
+        copy.wait()
+        onward.start()
+    for onward in outward:
+        onward.wait()
+
+
+def settled(a, b):
     anywhere = pl.BlockSpec(memory_space=pl.ANY)
-    inner = pl.BlockSpec(memory_space=space)
     return pl.pallas_call(
         settle,
         out_shape=(jax.ShapeDtypeStruct(a.shape, a.dtype), jax.ShapeDtypeStruct(b.shape, b.dtype)),
-        in_specs=[inner, inner],
+        in_specs=[anywhere, anywhere],
         out_specs=(anywhere, anywhere),
-        scratch_shapes=[pltpu.SemaphoreType.DMA((2,))],
+        scratch_shapes=[
+            pltpu.VMEM(a.shape, a.dtype),
+            pltpu.VMEM(b.shape, b.dtype),
+            pltpu.SemaphoreType.DMA((2, 1 + b.shape[0])),
+        ],
+        compiler_params=pltpu.CompilerParams(vmem_limit_bytes=56 * 1024 * 1024),
     )(a, b)
 
 

time: 27 us -> 26.8 us (level)
  Pallas kernels: 26.2 us -> 25.9 us
where the time goes in v4:
time: 26.8 us; the launch traced here: 26.6 us
  Pallas kernels  25.9 us (97%)
  between operations  0.64 us (2%)
    pallas_call x1, Pallas kernels, shards(): pl.pallas_call(functools.partial(body, sizes), out_shape=(jax.ShapeDtypeS...  24.3 us
    pallas_call x1, Pallas kernels, settled(): pl.pallas_call(settle, out_shape=(jax.ShapeDtypeStruct(a.shape, a.dtype),...  1.67 us

profile of v4, /device:TPU:0, one launch (start us, length us, event | category | flops | bytes accessed | tf_op | source)
XLA Modules:
  0.0 26.6 jit_solution(904223614812276705)
XLA Ops:
  0.6 24.3 %shard_map.104 = (bf16[4,4096]{1,0:T(4,128)(2,1)}, bf16[4,64,512]{2,1,0:T(8,128)(2,1)}) custom-call(bf16[8,2048]{1,0:T(8,128)(2,1)} %x.1, s32[2,8]{1,0:T(2,128)} %bitcast.10, f32[2,8]{1,0:T(2,128)} %bitcast.11, bf16[2048,512]{1,0:T(8,128)(2,1)} %bitcast.6, bf16[2048,512]{1,0:T(8,128)(2,1)} %bitcast.7, bf16[1024,1024]{1,0:T(8,128)(2,1)} %bitcast.8, ...), custom_call_target="tpu_custom_call" | custom-call | flops 402653184 | bytes 8388608 | tf_op jit(solution)/shard_map/pallas_call | solution.py:287
  24.9 1.7 %shard_map.105 = (bf16[4,4096]{1,0:T(4,128)(2,1)}, bf16[4,64,512]{2,1,0:T(8,128)(2,1)}) custom-call(bf16[4,4096]{1,0:T(4,128)(2,1)} %get-tuple-element.4.a, bf16[4,64,512]{2,1,0:T(8,128)(2,1)} %get-tuple-element.5.b), custom_call_target="tpu_custom_call" | custom-call | tf_op jit(solution)/shard_map/pallas_call | solution.py:348
